TPU v7x, 128 devices: a whole 4x4x4 slice. The times are simulated.
128 devices in a mesh: ctx: 32 (over z, x, core), head: 4 (over y).
Axes of the slice: x: 4, y: 4, z: 4, core: 2. Of those that a mesh axis runs over, the one named last changes fastest.
Arguments:
- queries: bfloat16 [32768, 4096], P('ctx', 'head'), may hold values from -12 to 12
- keys: bfloat16 [32768, 4096], P('ctx', 'head'), may hold values from -9 to 9
- values: bfloat16 [32768, 4096], P('ctx', 'head'), may hold values from -6 to 6
- w_out: bfloat16 [4096, 4096], P('head'), may hold values from -0.125 to 0.125
Outputs:
- mixed: bfloat16 [32768, 4096], P('ctx', 'head')
All inputs are finite; a program needn't handle non-finite values.
Results may differ from a plain program's by a relative error of at most 0.013.
Values may be sent and summed in bfloat16 or wider, within the bound.
A program may use at most 192 MiB of HBM per device.

v0:
```python
import math

import jax
import jax.numpy as jnp
from jax import lax
from jax.experimental import pallas as pl
from jax.experimental.pallas import tpu as pltpu
from jax.sharding import PartitionSpec as P

MESH = pl.DeviceIdType.MESH
DH = 128
HEADS_HERE = 8
ROWS = 1024
COLS = 1024
MID = 128
TOP = 32
R_MID = 8
R_TOP = 32
QB = 256
NEG = -1e30
COEF = DH ** -0.5 / math.log(2.0)
F32 = jnp.float32
BF16 = jnp.bfloat16


def dot_t(a, b):
    return lax.dot_general(a, b, (((1,), (1,)), ((), ())), preferred_element_type=F32)


def dot(a, b):
    return jnp.dot(a, b, preferred_element_type=F32)


class Ring:
    def __init__(self, copy, plus, minus, own, far_plus, far_minus):
        self.first = [copy(*own[0], plus), copy(*own[1], minus)]
        self.second = [copy(*far_plus, plus), copy(*far_minus, minus)]

    def start(self):
        for one in self.first:
            one.start()

    def forward(self):
        for came, onward in zip(self.first, self.second):
            came.wait_recv()
            onward.start()

    def finish(self):
        for one in self.second:
            one.wait_recv()

    def drain(self):
        for one in self.first + self.second:
            one.wait_send()


def body(q_hbm, k_hbm, v_hbm, w_hbm, out_hbm,
         q, k, v, wc_own, wo_own, attn, attn_p, mid, top, wc, wo, rs_s, rs_r, out,
         patch, patch_p, qa, qt, wide, m0, l0, n0, aff, tops, send, recv, lsem):
    place = lax.axis_index("ctx")
    h = lax.axis_index("head")
    z = lax.div(place, 8)
    x = lax.rem(lax.div(place, 2), 4)
    c = lax.rem(place, 2)
    near = h + 1 - 2 * lax.rem(h, 2)
    pair = (1 - c) * near + c * (3 - h)
    cross = c * near + (1 - c) * (3 - h)
    diag = lax.rem(h + 2, 4)

    def at(zz, xx, cc):
        return lax.rem(zz, 4) * 8 + lax.rem(xx, 4) * 2 + cc

    xp, xm = (at(z, x + 1, c), h), (at(z, x + 3, c), h)
    zp, zm = (at(z + 1, x, c), h), (at(z + 3, x, c), h)
    sib = (at(z, x, 1 - c), h)
    dp, dc = (place, pair), (place, cross)

    count = [0]

    def copy(src, dst, device):
        i = count[0]
        count[0] += 1
        return pltpu.make_async_remote_copy(
            src_ref=src, dst_ref=dst, send_sem=send.at[i], recv_sem=recv.at[i],
            device_id=device, device_id_type=MESH)

    lcount = [0]

    def load(src, dst):
        i = lcount[0]
        lcount[0] += 1
        return pltpu.make_async_copy(src, dst, lsem.at[i])

    xl, xr = lax.rem(x + 3, 4), lax.rem(x + 1, 4)

    k_load, v_load, q_load = load(k_hbm, k), load(v_hbm, v), load(q_hbm, q)
    for one in (k_load, v_load, q_load):
        one.start()

    barrier = pltpu.get_barrier_semaphore()
    for other in (xp, xm, zp, zm, sib, dp, dc):
        pl.semaphore_signal(barrier, inc=1, device_id=other, device_id_type=MESH)
    pl.semaphore_wait(barrier, 7)

    def w_piece(block):
        return w_hbm.at[pl.ds(pl.multiple_of(x * 256, 256), 256),
                        pl.ds(pl.multiple_of(block * COLS + z * 256, 256), 256)]

    wc_hop = copy(w_piece(diag), wc.at[0, x], dp)
    wo_hop = copy(w_piece(pair), wo.at[x, 0], dp)
    wc_hop.start()
    wo_hop.start()

    wc_x = Ring(copy, xp, xm,
                [(wc.at[0, x], wc.at[0, x])] * 2,
                (wc.at[0, xl, pl.ds(0, 128)], wc.at[0, xl, pl.ds(0, 128)]),
                (wc.at[0, xr, pl.ds(128, 128)], wc.at[0, xr, pl.ds(128, 128)]))
    wc_z = Ring(copy, zp, zm,
                [(wc.at[0], wc.at[3]), (wc.at[0], wc.at[1])],
                (wc.at[3, pl.ds(0, 2)], wc.at[2, pl.ds(0, 2)]),
                (wc.at[1, pl.ds(2, 2)], wc.at[2, pl.ds(2, 2)]))
    wo_z = Ring(copy, zp, zm,
                [(wo.at[x, 0], wo.at[x, 3]), (wo.at[x, 0], wo.at[x, 1])],
                (wo.at[x, 3, pl.ds(0, 128)], wo.at[x, 2, pl.ds(0, 128)]),
                (wo.at[x, 1, pl.ds(128, 128)], wo.at[x, 2, pl.ds(128, 128)]))
    wo_x = Ring(copy, xp, xm,
                [(wo.at[x], wo.at[x])] * 2,
                (wo.at[xl, pl.ds(0, 2)], wo.at[xl, pl.ds(0, 2)]),
                (wo.at[xr, pl.ds(2, 2)], wo.at[xr, pl.ds(2, 2)]))
    mid_x = Ring(copy, xp, xm,
                 [(mid.at[x, c], mid.at[x, c])] * 2,
                 (mid.at[xl, c, 0], mid.at[xl, c, 0]),
                 (mid.at[xr, c, 1], mid.at[xr, c, 1]))
    top_x = Ring(copy, xp, xm,
                 [(top.at[0, c, x], top.at[0, c, x])] * 2,
                 (top.at[0, c, xl, 0], top.at[0, c, xl, 0]),
                 (top.at[0, c, xr, 1], top.at[0, c, xr, 1]))
    top_z = Ring(copy, zp, zm,
                 [(top.at[0, c], top.at[3, c]), (top.at[0, c], top.at[1, c])],
                 (top.at[3, c, pl.ds(0, 2)], top.at[2, c, pl.ds(0, 2)]),
                 (top.at[1, c, pl.ds(2, 2)], top.at[2, c, pl.ds(2, 2)]))
    mid_sib = [copy(mid.at[lax.rem(x + d, 4), c], mid.at[lax.rem(x + d, 4), c], sib) for d in range(4)]
    top_sib = [copy(top.at[d, c], top.at[d, c], sib) for d in range(4)]

    def select(src, cols, j):
        wide[...] = src[:, cols].astype(F32)
        rows = wide[pl.ds(j, MID, stride=R_MID), :]
        few = wide[pl.ds(h * 8 + j, TOP, stride=R_TOP), :]
        return rows.astype(BF16), few.astype(BF16)

    def pick(j, carry):
        cols = pl.ds(pl.multiple_of(j * DH, DH), DH)
        for kv, src in enumerate((k, v)):
            rows, few = select(src, cols, j)
            mid[x, c, kv, j] = rows
            top[0, c, x, kv, j] = few
        return carry

    k_load.wait()
    v_load.wait()
    lax.fori_loop(0, HEADS_HERE, pick, 0)
    top_x.start()
    mid_x.start()
    mid_sib[0].start()

    w_loads = []
    for d in range(4):
        zc = lax.rem(z + d, 4) * 256
        for block, dst in ((cross, wc_own), (h, wo_own)):
            w_loads.append(load(w_hbm.at[:, pl.ds(pl.multiple_of(block * COLS + zc, 256), 256)], dst.at[d]))
    for one in w_loads:
        one.start()

    base = count[0]
    count[0] += HEADS_HERE
    tri = lax.broadcasted_iota(jnp.int32, (QB, QB), 0) >= lax.broadcasted_iota(jnp.int32, (QB, QB), 1)

    def attn_send(j):
        cols = pl.ds(pl.multiple_of(j * DH, DH), DH)
        return pltpu.make_async_remote_copy(
            src_ref=attn.at[:, cols], dst_ref=attn_p.at[:, cols],
            send_sem=send.at[base + j], recv_sem=recv.at[base + j],
            device_id=dp, device_id_type=MESH)

    def level0(j, carry):
        cols = pl.ds(pl.multiple_of(j * DH, DH), DH)
        rows, few = select(q, cols, j)
        qa[j] = rows
        qt[j] = few
        vx = jnp.concatenate([v[:, cols], jnp.ones((ROWS, DH), BF16)], axis=1)
        for i in range(ROWS // QB):
            here = pl.ds(i * QB, QB)
            qi = q[here, cols]
            s_d = jnp.where(tri, dot_t(qi, k[here, cols]), NEG)
            peak = jnp.max(s_d, axis=1, keepdims=True)
            if i:
                s_o = dot_t(qi, k[pl.ds(0, i * QB), cols])
                peak = jnp.maximum(peak, jnp.max(s_o, axis=1, keepdims=True))
            p_d = jnp.exp2((s_d - peak) * COEF).astype(BF16)
            acc = dot(p_d, vx[i * QB:(i + 1) * QB])
            if i:
                p_o = jnp.exp2((s_o - peak) * COEF).astype(BF16)
                acc = acc + dot(p_o, vx[:i * QB])
            numer, total = acc[:, :DH], acc[:, DH:]
            m0[here] = jnp.broadcast_to(peak, (QB, DH))
            n0[here] = numer
            l0[here] = total
            attn[here, cols] = (numer / total).astype(BF16)
        picked = pl.ds(j, MID, stride=R_MID)
        aff[j, 0] = m0[picked, :]
        aff[j, 1] = l0[picked, :]
        aff[j, 2] = n0[picked, :]
        attn_send(j).start()
        return carry

    q_load.wait()
    lax.fori_loop(0, 2, level0, 0)
    wc_hop.wait_recv()
    wo_hop.wait_recv()
    wc_x.start()
    wo_z.start()
    top_x.forward()
    lax.fori_loop(2, 5, level0, 0)
    top_x.finish()
    top_z.start()
    top_sib[0].start()
    lax.fori_loop(5, 8, level0, 0)
    mid_x.forward()
    mid_sib[1].start()
    mid_sib[3].start()
    wc_x.forward()
    wo_z.forward()
    mid_x.finish()
    mid_sib[2].start()
    wc_x.finish()
    wc_z.start()
    top_z.forward()
    top_sib[1].start()
    top_sib[3].start()
    wo_z.finish()
    wo_x.start()
    top_z.finish()
    top_sib[2].start()
    for one in mid_sib + top_sib:
        one.wait_recv()

    def late(j, carry):
        def attend(qs, key, val, ok):
            s = jnp.where(ok, dot_t(qs, key), NEG)
            peak = jnp.max(s, axis=1, keepdims=True)
            p = jnp.exp2((s - peak) * COEF).astype(BF16)
            acc = dot(p, jnp.concatenate([val, jnp.ones((1024, DH), BF16)], axis=1))
            return jnp.broadcast_to(peak, (qs.shape[0], DH)), acc[:, DH:], acc[:, :DH]

        row = lax.broadcasted_iota(jnp.int32, (MID, 1024), 0)
        col = lax.broadcasted_iota(jnp.int32, (MID, 1024), 1)
        m1, l1, n1 = attend(qa[j], mid[:, :, 0, j].reshape(1024, DH), mid[:, :, 1, j].reshape(1024, DH),
                            col <= row + (x * 2 + c) * MID)
        row = lax.broadcasted_iota(jnp.int32, (TOP, 1024), 0)
        col = lax.broadcasted_iota(jnp.int32, (TOP, 1024), 1)
        kz = (z + (col >> 8)) & 3
        spot = ((kz * 8 + ((col >> 5) & 3) * 2 + ((col >> 7) & 1)) * TOP) + (col & 31)
        m2, l2, n2 = attend(qt[j], top[:, :, :, 0, j].reshape(1024, DH), top[:, :, :, 1, j].reshape(1024, DH),
                            spot <= row + place * TOP)
        tops[0] = jnp.full((MID, DH), NEG, F32)
        tops[1] = jnp.zeros((MID, DH), F32)
        tops[2] = jnp.zeros((MID, DH), F32)
        hit = pl.ds(h, TOP, stride=4)
        tops[0, hit, :] = m2
        tops[1, hit, :] = l2
        tops[2, hit, :] = n2
        ma, mt = aff[j, 0], tops[0]
        peak = jnp.maximum(ma, jnp.maximum(m1, mt))
        fa = jnp.exp2((ma - peak) * COEF)
        fm = jnp.exp2((m1 - peak) * COEF)
        ft = jnp.exp2((mt - peak) * COEF)
        upper = aff[j, 2] * fa + n1 * fm + tops[2] * ft
        lower = aff[j, 1] * fa + l1 * fm + tops[1] * ft
        patch[j] = (upper / lower).astype(BF16)
        return carry

    lax.fori_loop(0, HEADS_HERE, late, 0)
    patch_send = copy(patch, patch_p, dp)
    patch_send.start()

    def mend(target, source):
        def one(j, carry):
            cols = pl.ds(pl.multiple_of(j * DH, DH), DH)
            old = target[:, cols].astype(F32).reshape(MID, R_MID, DH)
            new = source[j].astype(F32).reshape(MID, 1, DH)
            lane = lax.broadcasted_iota(jnp.int32, (MID, R_MID, DH), 1)
            target[:, cols] = jnp.where(lane == j, new, old).reshape(ROWS, DH).astype(BF16)
            return carry
        lax.fori_loop(0, HEADS_HERE, one, 0)

    for j in range(HEADS_HERE):
        attn_send(j).wait_send()
    mend(attn, patch)
    wc_z.forward()
    wo_x.forward()
    for j in range(HEADS_HERE):
        attn_send(j).wait_recv()
    patch_send.wait_recv()
    mend(attn_p, patch_p)

    for one in w_loads:
        one.wait()
    HALF = ROWS // 2
    sums = []
    for d in (0, 1, 3, 2):
        if d == 2:
            wc_z.finish()
        for part in range(2):
            here = pl.ds(part * HALF, HALF)
            rs_s[d, here] = (dot(attn[here], wc_own[d])
                             + dot(attn_p[here], wc[d].reshape(1024, 256))).astype(BF16)
            one = copy(rs_s.at[d, here], rs_r.at[d, here], dc)
            one.start()
            sums.append((d, here, one))
    wo_x.finish()
    stores = []
    for d, here, one in sums:
        mine = dot(attn[here], wo_own[d]) + dot(attn_p[here], wo[:, d].reshape(1024, 256))
        one.wait_recv()
        out[d, here] = (mine + rs_r[d, here].astype(F32)).astype(BF16)
        zc = pl.multiple_of(lax.rem(z + d, 4) * 256, 256)
        stores.append(load(out.at[d, here], out_hbm.at[here, pl.ds(zc, 256)]))
        stores[-1].start()

    for ring in (wc_x, wc_z, wo_z, wo_x, mid_x, top_x, top_z):
        ring.drain()
    for one in mid_sib + top_sib + [wc_hop, wo_hop, patch_send] + [s[2] for s in sums]:
        one.wait_send()
    for one in stores:
        one.wait()


def local(queries, keys, values, w_out):
    any_space = pl.BlockSpec(memory_space=pl.ANY)
    vm = pltpu.VMEM
    return pl.pallas_call(
        body,
        name="attend",
        out_shape=jax.ShapeDtypeStruct((ROWS, COLS), BF16),
        in_specs=[any_space] * 4,
        out_specs=any_space,
        scratch_shapes=[
            vm((ROWS, COLS), BF16), vm((ROWS, COLS), BF16), vm((ROWS, COLS), BF16),
            vm((4, 1024, 256), BF16), vm((4, 1024, 256), BF16),
            vm((ROWS, COLS), BF16), vm((ROWS, COLS), BF16),
            vm((4, 2, 2, 8, MID, DH), BF16),
            vm((4, 2, 4, 2, 8, TOP, DH), BF16),
            vm((4, 4, 256, 256), BF16), vm((4, 4, 256, 256), BF16),
            vm((4, ROWS, 256), BF16), vm((4, ROWS, 256), BF16), vm((4, ROWS, 256), BF16),
            vm((8, MID, DH), BF16), vm((8, MID, DH), BF16),
            vm((8, MID, DH), BF16), vm((8, TOP, DH), BF16),
            vm((ROWS, DH), F32), vm((ROWS, DH), F32), vm((ROWS, DH), F32), vm((ROWS, DH), F32),
            vm((8, 3, MID, DH), F32), vm((3, MID, DH), F32),
            pltpu.SemaphoreType.DMA((64,)), pltpu.SemaphoreType.DMA((64,)),
            pltpu.SemaphoreType.DMA((24,)),
        ],
        cost_estimate=pl.CostEstimate(flops=15_000_000_000, bytes_accessed=24_000_000, transcendentals=8_000_000),
        compiler_params=pltpu.CompilerParams(
            collective_id=0, has_side_effects=True, vmem_limit_bytes=56 * 2 ** 20),
    )(queries, keys, values, w_out)


def solution(mesh):
    placed = (P("ctx", "head"), P("ctx", "head"), P("ctx", "head"), P("head", None))
    return jax.shard_map(
        local, mesh=mesh, in_specs=placed, out_specs=P("ctx", "head"), check_vma=False
    )
```

profile of v0, /device:TPU:0, one launch (start us, length us, event | category | flops | bytes accessed | tf_op | source)
XLA Modules:
  0.0 105.2 jit_solution(10014663849119212439)
XLA Ops:
  0.0 102.1 %attend.1 = bf16[1024,1024]{1,0:T(8,128)(2,1)} custom-call(bf16[1024,1024]{1,0:T(8,128)(2,1)} %q_hbm.1, bf16[1024,1024]{1,0:T(8,128)(2,1)} %k_hbm.1, bf16[1024,1024]{1,0:T(8,128)(2,1)} %v_hbm.1, bf16[1024,4096]{1,0:T(8,128)(2,1)} %w_hbm.1), custom_call_target="tpu_custom_call" | custom-call | flops 15000000512 | bytes 24000000 | tf_op jit(solution)/shard_map/attend/pallas_call | solution.py:341
  102.1 3.1 %copy.6 = bf16[1024,1024]{1,0:T(8,128)(2,1)} copy(bf16[1024,1024]{1,0:T(8,128)(2,1)} %attend.1) | data formatting | bytes 4194304
where the time goes:
time: 106 us; the launch traced here: 105 us
  Pallas kernels  102 us (96%)
  local copies, waits for them, and re-layouts  3.08 us (3%)
    pallas_call x1, Pallas kernels, local(): pl.pallas_call(body, name='attend', out_shape=jax.ShapeDtypeStruct((ROWS,...  102 us
    unnamed x1, local copies, waits for them, and re-layouts  3.08 us

commit v1 on v0

v1 whole, which is shorter than its diff:
```python
import math

import jax
import jax.numpy as jnp
from jax import lax
from jax.experimental import pallas as pl
from jax.experimental.pallas import tpu as pltpu
from jax.sharding import PartitionSpec as P

MESH = pl.DeviceIdType.MESH
DH = 128
HEADS_HERE = 8
ROWS = 1024
COLS = 1024
MID = 128
TOP = 32
R_MID = 8
R_TOP = 32
QB = 256
NEG = -1e30
COEF = DH ** -0.5 / math.log(2.0)
F32 = jnp.float32
BF16 = jnp.bfloat16


def dot_t(a, b):
    return lax.dot_general(a, b, (((1,), (1,)), ((), ())), preferred_element_type=F32)


def dot(a, b):
    return jnp.dot(a, b, preferred_element_type=F32)


class Ring:
    def __init__(self, copy, plus, minus, own, far_plus, far_minus):
        self.first = [copy(*own[0], plus), copy(*own[1], minus)]
        self.second = [copy(*far_plus, plus), copy(*far_minus, minus)]

    def start(self):
        for one in self.first:
            one.start()

    def forward(self):
        for came, onward in zip(self.first, self.second):
            came.wait_recv()
            onward.start()

    def finish(self):
        for one in self.second:
            one.wait_recv()

    def drain(self):
        for one in self.first + self.second:
            one.wait_send()


def attend(qs, parts):
    scores = []
    for key, _, ok in parts:
        one = dot_t(qs, key)
        scores.append(one if ok is None else jnp.where(ok, one, NEG))
    peak = jnp.max(scores[0], axis=1, keepdims=True)
    for one in scores[1:]:
        peak = jnp.maximum(peak, jnp.max(one, axis=1, keepdims=True))
    acc = None
    for one, (_, val, _) in zip(scores, parts):
        term = dot(jnp.exp2((one - peak) * COEF).astype(BF16), val)
        acc = term if acc is None else acc + term
    total = acc[:, DH:]
    return acc[:, :DH] / total, jnp.broadcast_to(peak * COEF, total.shape) + jnp.log2(total)


def with_ones(val):
    return jnp.concatenate([val, jnp.ones(val.shape, BF16)], axis=1)


def body(q_hbm, k_hbm, v_hbm, w_hbm, out_hbm,
         q, k, v, wc_own, wo_own, attn, attn_p, wc, wo, rs_s, rs_r, out,
         patch, patch_p, st_mid, st_top, mid, top, res_mid, res_top, ret_mid, ret_top,
         wide, e0, o0, aff, spread, send, recv, lsem):
    place = lax.axis_index("ctx")
    h = lax.axis_index("head")
    z = lax.div(place, 8)
    x = lax.rem(lax.div(place, 2), 4)
    c = lax.rem(place, 2)
    s = x * 2 + c
    u = z * 2 + c
    near = h + 1 - 2 * lax.rem(h, 2)
    pair = (1 - c) * near + c * (3 - h)
    cross = c * near + (1 - c) * (3 - h)
    diag = lax.rem(h + 2, 4)

    def at(zz, xx, cc):
        return lax.rem(zz, 4) * 8 + lax.rem(xx, 4) * 2 + cc

    xp, xm = (at(z, x + 1, c), h), (at(z, x + 3, c), h)
    zp, zm = (at(z + 1, x, c), h), (at(z + 3, x, c), h)
    dp, dc = (place, pair), (place, cross)
    row_mates = [lax.rem(s + d, 8) for d in range(1, 8)]
    row_devs = [(z * 8 + t, h) for t in row_mates]
    col_mates = [lax.rem(u + d, 8) for d in range(1, 8)]
    col_devs = [(at(lax.div(t, 2), x, lax.rem(t, 2)), h) for t in col_mates]

    count = [0]

    def copy(src, dst, device):
        i = count[0]
        count[0] += 1
        return pltpu.make_async_remote_copy(
            src_ref=src, dst_ref=dst, send_sem=send.at[i], recv_sem=recv.at[i],
            device_id=device, device_id_type=MESH)

    lcount = [0]

    def load(src, dst):
        i = lcount[0]
        lcount[0] += 1
        return pltpu.make_async_copy(src, dst, lsem.at[i])

    xl, xr = lax.rem(x + 3, 4), lax.rem(x + 1, 4)

    loads = [load(q_hbm, q), load(k_hbm, k), load(v_hbm, v)]
    for one in loads:
        one.start()

    barrier = pltpu.get_barrier_semaphore()
    for other in row_devs + [(at(z + d, x, cc), h) for d in (1, 2, 3) for cc in (0, 1)] + [dp, dc]:
        pl.semaphore_signal(barrier, inc=1, device_id=other, device_id_type=MESH)

    w_loads = []
    for d in range(4):
        zc = lax.rem(z + d, 4) * 256
        for block, dst in ((cross, wc_own), (h, wo_own)):
            w_loads.append(load(w_hbm.at[:, pl.ds(pl.multiple_of(block * COLS + zc, 256), 256)], dst.at[d]))

    def pick(j, carry):
        cols = pl.ds(pl.multiple_of(j * DH, DH), DH)
        for i, src in enumerate((q, k, v)):
            wide[...] = src[:, cols].astype(F32)
            st_mid[j, i] = wide[pl.ds(j, MID, stride=R_MID), :].astype(BF16)
            st_top[j, i] = wide[pl.ds(h * 8 + j, TOP, stride=R_TOP), :].astype(BF16)
        return carry

    for one in loads:
        one.wait()
    lax.fori_loop(0, HEADS_HERE, pick, 0)
    mid[s] = st_mid[s]
    top[x, :, u] = st_top[u]
    pl.semaphore_wait(barrier, 15)

    mid_go = [copy(st_mid.at[t], mid.at[s], one) for t, one in zip(row_mates, row_devs)]
    top_go = [copy(st_top.at[t], top.at[x, :, u], one) for t, one in zip(col_mates, col_devs)]
    mid_back = [copy(res_mid.at[t], ret_mid.at[s], one) for t, one in zip(row_mates, row_devs)]
    top_back = [copy(res_top.at[t], ret_top.at[u], one) for t, one in zip(col_mates, col_devs)]

    def w_piece(block):
        return w_hbm.at[pl.ds(pl.multiple_of(x * 256, 256), 256),
                        pl.ds(pl.multiple_of(block * COLS + z * 256, 256), 256)]

    wc_hop = copy(w_piece(diag), wc.at[0, x], dp)
    wo_hop = copy(w_piece(pair), wo.at[x, 0], dp)
    top_x = Ring(copy, xp, xm,
                 [(top.at[x, pl.ds(1, 2)], top.at[x, pl.ds(1, 2)])] * 2,
                 (top.at[xl, 1], top.at[xl, 1]),
                 (top.at[xr, 2], top.at[xr, 2]))
    wc_x = Ring(copy, xp, xm,
                [(wc.at[0, x], wc.at[0, x])] * 2,
                (wc.at[0, xl, pl.ds(0, 128)], wc.at[0, xl, pl.ds(0, 128)]),
                (wc.at[0, xr, pl.ds(128, 128)], wc.at[0, xr, pl.ds(128, 128)]))
    wc_z = Ring(copy, zp, zm,
                [(wc.at[0], wc.at[3]), (wc.at[0], wc.at[1])],
                (wc.at[3, pl.ds(0, 2)], wc.at[2, pl.ds(0, 2)]),
                (wc.at[1, pl.ds(2, 2)], wc.at[2, pl.ds(2, 2)]))
    wo_z = Ring(copy, zp, zm,
                [(wo.at[x, 0], wo.at[x, 3]), (wo.at[x, 0], wo.at[x, 1])],
                (wo.at[x, 3, pl.ds(0, 128)], wo.at[x, 2, pl.ds(0, 128)]),
                (wo.at[x, 1, pl.ds(128, 128)], wo.at[x, 2, pl.ds(128, 128)]))
    wo_x = Ring(copy, xp, xm,
                [(wo.at[x], wo.at[x])] * 2,
                (wo.at[xl, pl.ds(0, 2)], wo.at[xl, pl.ds(0, 2)]),
                (wo.at[xr, pl.ds(2, 2)], wo.at[xr, pl.ds(2, 2)]))

    for one in top_go + mid_go + [wc_hop, wo_hop]:
        one.start()
    for one in w_loads:
        one.start()

    base = count[0]
    count[0] += HEADS_HERE
    tri = lax.broadcasted_iota(jnp.int32, (QB, QB), 0) >= lax.broadcasted_iota(jnp.int32, (QB, QB), 1)

    def attn_send(j):
        cols = pl.ds(pl.multiple_of(j * DH, DH), DH)
        return pltpu.make_async_remote_copy(
            src_ref=attn.at[:, cols], dst_ref=attn_p.at[:, cols],
            send_sem=send.at[base + j], recv_sem=recv.at[base + j],
            device_id=dp, device_id_type=MESH)

    def level0(j, carry):
        cols = pl.ds(pl.multiple_of(j * DH, DH), DH)
        vx = with_ones(v[:, cols])
        for i in range(ROWS // QB):
            here, past = pl.ds(i * QB, QB), pl.ds(0, i * QB)
            parts = [(k[here, cols], vx[i * QB:(i + 1) * QB], tri)]
            if i:
                parts.append((k[past, cols], vx[:i * QB], None))
            o, e = attend(q[here, cols], parts)
            o0[here] = o
            e0[here] = e
            attn[here, cols] = o.astype(BF16)
        picked = pl.ds(j, MID, stride=R_MID)
        aff[j, 0] = o0[picked, :]
        aff[j, 1] = e0[picked, :]
        attn_send(j).start()
        return carry

    def level1():
        for i in range(4):
            now = mid[2 * i:2 * i + 2]
            parts = [(now[:, 1].reshape(QB, DH), with_ones(now[:, 2].reshape(QB, DH)), tri)]
            if i:
                past = mid[0:2 * i]
                parts.append((past[:, 1].reshape(i * QB, DH), with_ones(past[:, 2].reshape(i * QB, DH)), None))
            o, e = attend(now[:, 0].reshape(QB, DH), parts)
            for half in range(2):
                res_mid[2 * i + half, pl.ds(0, MID)] = o[half * MID:(half + 1) * MID]
                res_mid[2 * i + half, pl.ds(MID, 8)] = e[half * MID:(half + 1) * MID].T[:8]

    def level2():
        row = lax.broadcasted_iota(jnp.int32, (256, 1024), 0)
        col = lax.broadcasted_iota(jnp.int32, (256, 1024), 1)

        def spot(index, xx):
            return (((index >> 6) & 3) * 8 + xx * 2 + ((index >> 5) & 1)) * TOP + (index & 31)

        ok = spot(col, col >> 8) <= spot(row, x)
        key = top[:, 1].reshape(1024, DH)
        val = top[:, 2].reshape(1024, DH)
        o, e = attend(top[x, 0].reshape(256, DH), [(key, with_ones(val), ok)])
        for t in range(8):
            res_top[t, 0] = o[t * TOP:(t + 1) * TOP]
            res_top[t, 1] = e[t * TOP:(t + 1) * TOP]

    lax.fori_loop(0, 2, level0, 0)
    wc_hop.wait_recv()
    wo_hop.wait_recv()
    wc_x.start()
    wo_z.start()
    for one in top_go:
        one.wait_recv()
    top_x.start()
    lax.fori_loop(2, 4, level0, 0)
    for one in mid_go:
        one.wait_recv()
    level1()
    for one in mid_back:
        one.start()
    ret_mid[s] = res_mid[s]
    top_x.forward()
    wc_x.forward()
    wo_z.forward()
    lax.fori_loop(4, 6, level0, 0)
    wc_x.finish()
    wc_z.start()
    wo_z.finish()
    wo_x.start()
    top_x.finish()
    level2()
    for one in top_back:
        one.start()
    ret_top[u] = res_top[u]
    lax.fori_loop(6, 8, level0, 0)

    for one in mid_back + top_back:
        one.wait_recv()

    def late(j, carry):
        spread[0] = jnp.zeros((MID, DH), F32)
        spread[1] = jnp.full((MID, DH), NEG, F32)
        hit = pl.ds(h, TOP, stride=4)
        spread[0, hit, :] = ret_top[j, 0]
        spread[1, hit, :] = ret_top[j, 1]
        ea, et = aff[j, 1], spread[1]
        em = jnp.broadcast_to(ret_mid[j, pl.ds(MID, 1)], (MID, DH)).T
        peak = jnp.maximum(ea, jnp.maximum(em, et))
        fa, fm, ft = jnp.exp2(ea - peak), jnp.exp2(em - peak), jnp.exp2(et - peak)
        upper = aff[j, 0] * fa + ret_mid[j, pl.ds(0, MID)] * fm + spread[0] * ft
        patch[j] = (upper / (fa + fm + ft)).astype(BF16)
        return carry

    lax.fori_loop(0, HEADS_HERE, late, 0)
    patch_send = copy(patch, patch_p, dp)
    patch_send.start()

    def mend(target, source):
        def one(j, carry):
            cols = pl.ds(pl.multiple_of(j * DH, DH), DH)
            old = target[:, cols].astype(F32).reshape(MID, R_MID, DH)
            new = source[j].astype(F32).reshape(MID, 1, DH)
            lane = lax.broadcasted_iota(jnp.int32, (MID, R_MID, DH), 1)
            target[:, cols] = jnp.where(lane == j, new, old).reshape(ROWS, DH).astype(BF16)
            return carry
        lax.fori_loop(0, HEADS_HERE, one, 0)

    wc_z.forward()
    wo_x.forward()
    for j in range(HEADS_HERE):
        attn_send(j).wait_send()
    mend(attn, patch)
    for j in range(HEADS_HERE):
        attn_send(j).wait_recv()
    patch_send.wait_recv()
    mend(attn_p, patch_p)

    for one in w_loads:
        one.wait()
    HALF = ROWS // 2
    sums = []
    for d in (0, 1, 3, 2):
        if d == 2:
            wc_z.finish()
        for part in range(2):
            here = pl.ds(part * HALF, HALF)
            rs_s[d, here] = (dot(attn[here], wc_own[d])
                             + dot(attn_p[here], wc[d].reshape(1024, 256))).astype(BF16)
            one = copy(rs_s.at[d, here], rs_r.at[d, here], dc)
            one.start()
            sums.append((d, here, one))
    wo_x.finish()
    stores = []
    for d, here, one in sums:
        mine = dot(attn[here], wo_own[d]) + dot(attn_p[here], wo[:, d].reshape(1024, 256))
        one.wait_recv()
        out[d, here] = (mine + rs_r[d, here].astype(F32)).astype(BF16)
        zc = pl.multiple_of(lax.rem(z + d, 4) * 256, 256)
        stores.append(load(out.at[d, here], out_hbm.at[here, pl.ds(zc, 256)]))
        stores[-1].start()

    for ring in (wc_x, wc_z, wo_z, wo_x, top_x):
        ring.drain()
    for one in mid_go + top_go + mid_back + top_back + [wc_hop, wo_hop, patch_send] + [t[2] for t in sums]:
        one.wait_send()
    for one in stores:
        one.wait()


def local(queries, keys, values, w_out):
    any_space = pl.BlockSpec(memory_space=pl.ANY)
    vm = pltpu.VMEM
    return pl.pallas_call(
        body,
        name="attend",
        out_shape=jax.ShapeDtypeStruct((ROWS, COLS), BF16),
        in_specs=[any_space] * 4,
        out_specs=any_space,
        scratch_shapes=[
            vm((ROWS, COLS), BF16), vm((ROWS, COLS), BF16), vm((ROWS, COLS), BF16),
            vm((4, 1024, 256), BF16), vm((4, 1024, 256), BF16),
            vm((ROWS, COLS), BF16), vm((ROWS, COLS), BF16),
            vm((4, 4, 256, 256), BF16), vm((4, 4, 256, 256), BF16),
            vm((4, ROWS, 256), BF16), vm((4, ROWS, 256), BF16), vm((4, ROWS, 256), BF16),
            vm((8, MID, DH), BF16), vm((8, MID, DH), BF16),
            vm((8, 3, MID, DH), BF16), vm((8, 3, TOP, DH), BF16),
            vm((8, 3, MID, DH), BF16), vm((4, 3, 8, TOP, DH), BF16),
            vm((8, MID + 8, DH), F32), vm((8, 2, TOP, DH), F32),
            vm((8, MID + 8, DH), F32), vm((8, 2, TOP, DH), F32),
            vm((ROWS, DH), F32), vm((ROWS, DH), F32), vm((ROWS, DH), F32),
            vm((8, 2, MID, DH), F32), vm((2, MID, DH), F32),
            pltpu.SemaphoreType.DMA((80,)), pltpu.SemaphoreType.DMA((80,)),
            pltpu.SemaphoreType.DMA((24,)),
        ],
        cost_estimate=pl.CostEstimate(flops=15_000_000_000, bytes_accessed=24_000_000, transcendentals=8_000_000),
        compiler_params=pltpu.CompilerParams(
            collective_id=0, has_side_effects=True, vmem_limit_bytes=56 * 2 ** 20),
    )(queries, keys, values, w_out)


def solution(mesh):
    placed = (P("ctx", "head"), P("ctx", "head"), P("ctx", "head"), P("head", None))
    return jax.shard_map(
        local, mesh=mesh, in_specs=placed, out_specs=P("ctx", "head"), check_vma=False
    )
```

time: 106 us -> 91 us (0.86)
  Pallas kernels: 102 us -> 87.8 us
    pallas_call x1, Pallas kernels: 102 us -> 87.8 us  [local(): pl.pallas_call(body, name='attend', out_shape=jax.ShapeDtypeStruct((ROWS,...]
where the time goes in v1:
time: 91 us; the launch traced here: 90.9 us
  Pallas kernels  87.8 us (96%)
  local copies, waits for them, and re-layouts  3.08 us (3%)
    pallas_call x1, Pallas kernels, local(): pl.pallas_call(body, name='attend', out_shape=jax.ShapeDtypeStruct((ROWS,...  87.8 us
    unnamed x1, local copies, waits for them, and re-layouts  3.08 us

profile of v1, /device:TPU:0, one launch (start us, length us, event | category | flops | bytes accessed | tf_op | source)
XLA Modules:
  0.0 90.9 jit_solution(7643744936196247405)
XLA Ops:
  0.0 87.8 %attend.1 = bf16[1024,1024]{1,0:T(8,128)(2,1)} custom-call(bf16[1024,1024]{1,0:T(8,128)(2,1)} %q_hbm.1, bf16[1024,1024]{1,0:T(8,128)(2,1)} %k_hbm.1, bf16[1024,1024]{1,0:T(8,128)(2,1)} %v_hbm.1, bf16[1024,4096]{1,0:T(8,128)(2,1)} %w_hbm.1), custom_call_target="tpu_custom_call" | custom-call | flops 15000000512 | bytes 24000000 | tf_op jit(solution)/shard_map/attend/pallas_call | solution.py:350
  87.8 3.1 %copy.6 = bf16[1024,1024]{1,0:T(8,128)(2,1)} copy(bf16[1024,1024]{1,0:T(8,128)(2,1)} %attend.1) | data formatting | bytes 4194304

commit v2 on v1

--- a/solution.py
+++ b/solution.py
@@ -76,8 +76,8 @@
 
 def body(q_hbm, k_hbm, v_hbm, w_hbm, out_hbm,
          q, k, v, wc_own, wo_own, attn, attn_p, wc, wo, rs_s, rs_r, out,
-         patch, patch_p, st_mid, st_top, mid, top, res_mid, res_top, ret_mid, ret_top,
-         wide, e0, o0, aff, spread, send, recv, lsem):
+         st_mid, st_top, mid, top, res_mid, res_top, ret_mid, ret_top,
+         wide, e0, o0, aff, spread, sums_f, send, recv, lsem):
     place = lax.axis_index("ctx")
     h = lax.axis_index("head")
     z = lax.div(place, 8)
@@ -186,14 +186,14 @@
         one.start()
 
     base = count[0]
-    count[0] += HEADS_HERE
+    count[0] += HEADS_HERE * R_MID
     tri = lax.broadcasted_iota(jnp.int32, (QB, QB), 0) >= lax.broadcasted_iota(jnp.int32, (QB, QB), 1)
 
-    def attn_send(j):
-        cols = pl.ds(pl.multiple_of(j * DH, DH), DH)
+    def attn_send(j, r):
+        spot = (pl.ds(pl.multiple_of(r * MID, MID), MID), pl.ds(pl.multiple_of(j * DH, DH), DH))
         return pltpu.make_async_remote_copy(
-            src_ref=attn.at[:, cols], dst_ref=attn_p.at[:, cols],
-            send_sem=send.at[base + j], recv_sem=recv.at[base + j],
+            src_ref=attn.at[spot], dst_ref=attn_p.at[spot],
+            send_sem=send.at[base + j * R_MID + r], recv_sem=recv.at[base + j * R_MID + r],
             device_id=dp, device_id_type=MESH)
 
     def level0(j, carry):
@@ -207,11 +207,17 @@
             o, e = attend(q[here, cols], parts)
             o0[here] = o
             e0[here] = e
-            attn[here, cols] = o.astype(BF16)
+        for r in range(R_MID):
+            attn[pl.ds(r * MID, MID), cols] = o0[pl.ds(r, MID, stride=R_MID), :].astype(BF16)
+
+        def leave(d, carry):
+            attn_send(j, lax.rem(j + d, R_MID)).start()
+            return carry
+
+        lax.fori_loop(1, R_MID, leave, 0)
         picked = pl.ds(j, MID, stride=R_MID)
         aff[j, 0] = o0[picked, :]
         aff[j, 1] = e0[picked, :]
-        attn_send(j).start()
         return carry
 
     def level1():
@@ -223,8 +229,12 @@
                 parts.append((past[:, 1].reshape(i * QB, DH), with_ones(past[:, 2].reshape(i * QB, DH)), None))
             o, e = attend(now[:, 0].reshape(QB, DH), parts)
             for half in range(2):
-                res_mid[2 * i + half, pl.ds(0, MID)] = o[half * MID:(half + 1) * MID]
-                res_mid[2 * i + half, pl.ds(MID, 8)] = e[half * MID:(half + 1) * MID].T[:8]
+                res_mid[2 * i + half, pl.ds(0, MID)] = o[half * MID:(half + 1) * MID].astype(BF16)
+                rest = e[half * MID:(half + 1) * MID].T[:16]
+                for n in range(3):
+                    piece = rest.astype(BF16)
+                    res_mid[2 * i + half, pl.ds(MID + 16 * n, 16)] = piece
+                    rest = rest - piece.astype(F32)
 
     def level2():
         row = lax.broadcasted_iota(jnp.int32, (256, 1024), 0)
@@ -242,13 +252,11 @@
             res_top[t, 1] = e[t * TOP:(t + 1) * TOP]
 
     lax.fori_loop(0, 2, level0, 0)
-    wc_hop.wait_recv()
-    wo_hop.wait_recv()
-    wc_x.start()
-    wo_z.start()
     for one in top_go:
         one.wait_recv()
     top_x.start()
+    wo_hop.wait_recv()
+    wo_z.start()
     lax.fori_loop(2, 4, level0, 0)
     for one in mid_go:
         one.wait_recv()
@@ -257,22 +265,24 @@
         one.start()
     ret_mid[s] = res_mid[s]
     top_x.forward()
-    wc_x.forward()
-    wo_z.forward()
+    wc_hop.wait_recv()
+    wc_x.start()
     lax.fori_loop(4, 6, level0, 0)
-    wc_x.finish()
-    wc_z.start()
-    wo_z.finish()
-    wo_x.start()
     top_x.finish()
     level2()
     for one in top_back:
         one.start()
     ret_top[u] = res_top[u]
+    wc_x.forward()
+    wo_z.forward()
     lax.fori_loop(6, 8, level0, 0)
+    wc_x.finish()
+    wc_z.start()
 
     for one in mid_back + top_back:
         one.wait_recv()
+    wo_z.finish()
+    wo_x.start()
 
     def late(j, carry):
         spread[0] = jnp.zeros((MID, DH), F32)
@@ -281,42 +291,32 @@
         spread[0, hit, :] = ret_top[j, 0]
         spread[1, hit, :] = ret_top[j, 1]
         ea, et = aff[j, 1], spread[1]
-        em = jnp.broadcast_to(ret_mid[j, pl.ds(MID, 1)], (MID, DH)).T
+        tail = [ret_mid[j, pl.ds(MID + 16 * n, 16)].astype(F32)[:1] for n in range(3)]
+        em = jnp.broadcast_to(tail[0] + tail[1] + tail[2], (MID, DH)).T
         peak = jnp.maximum(ea, jnp.maximum(em, et))
         fa, fm, ft = jnp.exp2(ea - peak), jnp.exp2(em - peak), jnp.exp2(et - peak)
-        upper = aff[j, 0] * fa + ret_mid[j, pl.ds(0, MID)] * fm + spread[0] * ft
-        patch[j] = (upper / (fa + fm + ft)).astype(BF16)
+        upper = aff[j, 0] * fa + ret_mid[j, pl.ds(0, MID)].astype(F32) * fm + spread[0] * ft
+        attn[pl.ds(pl.multiple_of(j * MID, MID), MID), pl.ds(pl.multiple_of(j * DH, DH), DH)] = (
+            upper / (fa + fm + ft)).astype(BF16)
+        attn_send(j, j).start()
         return carry
 
     lax.fori_loop(0, HEADS_HERE, late, 0)
-    patch_send = copy(patch, patch_p, dp)
-    patch_send.start()
-
-    def mend(target, source):
-        def one(j, carry):
-            cols = pl.ds(pl.multiple_of(j * DH, DH), DH)
-            old = target[:, cols].astype(F32).reshape(MID, R_MID, DH)
-            new = source[j].astype(F32).reshape(MID, 1, DH)
-            lane = lax.broadcasted_iota(jnp.int32, (MID, R_MID, DH), 1)
-            target[:, cols] = jnp.where(lane == j, new, old).reshape(ROWS, DH).astype(BF16)
-            return carry
-        lax.fori_loop(0, HEADS_HERE, one, 0)
-
-    wc_z.forward()
-    wo_x.forward()
-    for j in range(HEADS_HERE):
-        attn_send(j).wait_send()
-    mend(attn, patch)
-    for j in range(HEADS_HERE):
-        attn_send(j).wait_recv()
-    patch_send.wait_recv()
-    mend(attn_p, patch_p)
+
+    def came(n, carry):
+        attn_send(lax.div(n, R_MID), lax.rem(n, R_MID)).wait_recv()
+        return carry
+
+    lax.fori_loop(0, HEADS_HERE * R_MID, came, 0)
 
     for one in w_loads:
         one.wait()
     HALF = ROWS // 2
     sums = []
     for d in (0, 1, 3, 2):
+        if d == 1:
+            wc_z.forward()
+            wo_x.forward()
         if d == 2:
             wc_z.finish()
         for part in range(2):
@@ -325,21 +325,35 @@
                              + dot(attn_p[here], wc[d].reshape(1024, 256))).astype(BF16)
             one = copy(rs_s.at[d, here], rs_r.at[d, here], dc)
             one.start()
-            sums.append((d, here, one))
+            sums.append((d, part, one))
     wo_x.finish()
     stores = []
-    for d, here, one in sums:
+    for d, part, one in sums:
+        here = pl.ds(part * HALF, HALF)
         mine = dot(attn[here], wo_own[d]) + dot(attn_p[here], wo[:, d].reshape(1024, 256))
         one.wait_recv()
-        out[d, here] = (mine + rs_r[d, here].astype(F32)).astype(BF16)
-        zc = pl.multiple_of(lax.rem(z + d, 4) * 256, 256)
-        stores.append(load(out.at[d, here], out_hbm.at[here, pl.ds(zc, 256)]))
-        stores[-1].start()
+        both = mine + rs_r[d, here].astype(F32)
+        for n in range(4):
+            for lane in range(2):
+                sums_f[lane, pl.ds(part * 4 + n, MID, stride=R_MID), :] = both[n * MID:(n + 1) * MID,
+                                                                            lane * DH:(lane + 1) * DH]
+        if part:
+            for lane in range(2):
+                out[d, :, lane * DH:(lane + 1) * DH] = sums_f[lane].astype(BF16)
+            zc = pl.multiple_of(lax.rem(z + d, 4) * 256, 256)
+            stores.append(load(out.at[d], out_hbm.at[:, pl.ds(zc, 256)]))
+            stores[-1].start()
 
     for ring in (wc_x, wc_z, wo_z, wo_x, top_x):
         ring.drain()
-    for one in mid_go + top_go + mid_back + top_back + [wc_hop, wo_hop, patch_send] + [t[2] for t in sums]:
+    for one in mid_go + top_go + mid_back + top_back + [wc_hop, wo_hop] + [t[2] for t in sums]:
         one.wait_send()
+
+    def gone(n, carry):
+        attn_send(lax.div(n, R_MID), lax.rem(n, R_MID)).wait_send()
+        return carry
+
+    lax.fori_loop(0, HEADS_HERE * R_MID, gone, 0)
     for one in stores:
         one.wait()
 
@@ -359,14 +373,14 @@
             vm((ROWS, COLS), BF16), vm((ROWS, COLS), BF16),
             vm((4, 4, 256, 256), BF16), vm((4, 4, 256, 256), BF16),
             vm((4, ROWS, 256), BF16), vm((4, ROWS, 256), BF16), vm((4, ROWS, 256), BF16),
-            vm((8, MID, DH), BF16), vm((8, MID, DH), BF16),
             vm((8, 3, MID, DH), BF16), vm((8, 3, TOP, DH), BF16),
             vm((8, 3, MID, DH), BF16), vm((4, 3, 8, TOP, DH), BF16),
-            vm((8, MID + 8, DH), F32), vm((8, 2, TOP, DH), F32),
-            vm((8, MID + 8, DH), F32), vm((8, 2, TOP, DH), F32),
+            vm((8, MID + 48, DH), BF16), vm((8, 2, TOP, DH), F32),
+            vm((8, MID + 48, DH), BF16), vm((8, 2, TOP, DH), F32),
             vm((ROWS, DH), F32), vm((ROWS, DH), F32), vm((ROWS, DH), F32),
             vm((8, 2, MID, DH), F32), vm((2, MID, DH), F32),
-            pltpu.SemaphoreType.DMA((80,)), pltpu.SemaphoreType.DMA((80,)),
+            vm((2, ROWS, DH), F32),
+            pltpu.SemaphoreType.DMA((144,)), pltpu.SemaphoreType.DMA((144,)),
             pltpu.SemaphoreType.DMA((24,)),
         ],
         cost_estimate=pl.CostEstimate(flops=15_000_000_000, bytes_accessed=24_000_000, transcendentals=8_000_000),

time: 91 us -> 79.3 us (0.87)
  Pallas kernels: 87.8 us -> 76 us
    pallas_call x1, Pallas kernels: 87.8 us -> 76 us  [local(): pl.pallas_call(body, name='attend', out_shape=jax.ShapeDtypeStruct((ROWS,...]
where the time goes in v2:
time: 79.3 us; the launch traced here: 79.1 us
  Pallas kernels  76 us (96%)
  local copies, waits for them, and re-layouts  3.08 us (4%)
    pallas_call x1, Pallas kernels, local(): pl.pallas_call(body, name='attend', out_shape=jax.ShapeDtypeStruct((ROWS,...  76 us
    unnamed x1, local copies, waits for them, and re-layouts  3.08 us

profile of v2, /device:TPU:0, one launch (start us, length us, event | category | flops | bytes accessed | tf_op | source)
XLA Modules:
  0.0 79.1 jit_solution(11622339584259561480)
XLA Ops:
  0.0 76.0 %attend.1 = bf16[1024,1024]{1,0:T(8,128)(2,1)} custom-call(bf16[1024,1024]{1,0:T(8,128)(2,1)} %q_hbm.1, bf16[1024,1024]{1,0:T(8,128)(2,1)} %k_hbm.1, bf16[1024,1024]{1,0:T(8,128)(2,1)} %v_hbm.1, bf16[1024,4096]{1,0:T(8,128)(2,1)} %w_hbm.1), custom_call_target="tpu_custom_call" | custom-call | flops 15000000512 | bytes 24000000 | tf_op jit(solution)/shard_map/attend/pallas_call | solution.py:364
  76.1 3.1 %copy.6 = bf16[1024,1024]{1,0:T(8,128)(2,1)} copy(bf16[1024,1024]{1,0:T(8,128)(2,1)} %attend.1) | data formatting | bytes 4194304

commit v3 on v2

--- a/solution.py
+++ b/solution.py
@@ -76,15 +76,14 @@
 
 def body(q_hbm, k_hbm, v_hbm, w_hbm, out_hbm,
          q, k, v, wc_own, wo_own, attn, attn_p, wc, wo, rs_s, rs_r, out,
-         st_mid, st_top, mid, top, res_mid, res_top, ret_mid, ret_top,
-         wide, e0, o0, aff, spread, sums_f, send, recv, lsem):
+         st_mid, st_top, mid, top, res_mid, ret_mid,
+         wide, e0, o0, aff, extra, sums_f, send, recv, lsem):
     place = lax.axis_index("ctx")
     h = lax.axis_index("head")
     z = lax.div(place, 8)
     x = lax.rem(lax.div(place, 2), 4)
     c = lax.rem(place, 2)
     s = x * 2 + c
-    u = z * 2 + c
     near = h + 1 - 2 * lax.rem(h, 2)
     pair = (1 - c) * near + c * (3 - h)
     cross = c * near + (1 - c) * (3 - h)
@@ -98,8 +97,6 @@
     dp, dc = (place, pair), (place, cross)
     row_mates = [lax.rem(s + d, 8) for d in range(1, 8)]
     row_devs = [(z * 8 + t, h) for t in row_mates]
-    col_mates = [lax.rem(u + d, 8) for d in range(1, 8)]
-    col_devs = [(at(lax.div(t, 2), x, lax.rem(t, 2)), h) for t in col_mates]
 
     count = [0]
 
@@ -118,13 +115,14 @@
         return pltpu.make_async_copy(src, dst, lsem.at[i])
 
     xl, xr = lax.rem(x + 3, 4), lax.rem(x + 1, 4)
+    zl, zr = lax.rem(z + 3, 4), lax.rem(z + 1, 4)
 
     loads = [load(q_hbm, q), load(k_hbm, k), load(v_hbm, v)]
     for one in loads:
         one.start()
 
     barrier = pltpu.get_barrier_semaphore()
-    for other in row_devs + [(at(z + d, x, cc), h) for d in (1, 2, 3) for cc in (0, 1)] + [dp, dc]:
+    for other in row_devs + [zp, zm, dp, dc]:
         pl.semaphore_signal(barrier, inc=1, device_id=other, device_id_type=MESH)
 
     w_loads = []
@@ -145,42 +143,35 @@
         one.wait()
     lax.fori_loop(0, HEADS_HERE, pick, 0)
     mid[s] = st_mid[s]
-    top[x, :, u] = st_top[u]
-    pl.semaphore_wait(barrier, 15)
+    top[z, :, s] = st_top[s]
+    extra[0] = jnp.zeros((ROWS, DH), F32)
+    extra[1] = jnp.full((ROWS, DH), NEG, F32)
+    pl.semaphore_wait(barrier, 11)
 
     mid_go = [copy(st_mid.at[t], mid.at[s], one) for t, one in zip(row_mates, row_devs)]
-    top_go = [copy(st_top.at[t], top.at[x, :, u], one) for t, one in zip(col_mates, col_devs)]
+    top_go = [copy(st_top.at[t], top.at[z, :, s], one) for t, one in zip(row_mates, row_devs)]
     mid_back = [copy(res_mid.at[t], ret_mid.at[s], one) for t, one in zip(row_mates, row_devs)]
-    top_back = [copy(res_top.at[t], ret_top.at[u], one) for t, one in zip(col_mates, col_devs)]
-
-    def w_piece(block):
-        return w_hbm.at[pl.ds(pl.multiple_of(x * 256, 256), 256),
-                        pl.ds(pl.multiple_of(block * COLS + z * 256, 256), 256)]
-
-    wc_hop = copy(w_piece(diag), wc.at[0, x], dp)
-    wo_hop = copy(w_piece(pair), wo.at[x, 0], dp)
-    top_x = Ring(copy, xp, xm,
-                 [(top.at[x, pl.ds(1, 2)], top.at[x, pl.ds(1, 2)])] * 2,
-                 (top.at[xl, 1], top.at[xl, 1]),
-                 (top.at[xr, 2], top.at[xr, 2]))
-    wc_x = Ring(copy, xp, xm,
-                [(wc.at[0, x], wc.at[0, x])] * 2,
-                (wc.at[0, xl, pl.ds(0, 128)], wc.at[0, xl, pl.ds(0, 128)]),
-                (wc.at[0, xr, pl.ds(128, 128)], wc.at[0, xr, pl.ds(128, 128)]))
+
+    def w_piece(block, n, d):
+        return w_hbm.at[pl.ds(pl.multiple_of(n * 256, 256), 256),
+                        pl.ds(pl.multiple_of(block * COLS + lax.rem(z + d, 4) * 256, 256), 256)]
+
+    wc_hop = [copy(w_piece(diag, n, 0), wc.at[0, n], dp) for n in range(4)]
+    wo_hop = [copy(w_piece(pair, x, d), wo.at[x, d], dp) for d in range(4)]
+    top_z = Ring(copy, zp, zm,
+                 [(top.at[z, pl.ds(1, 2)], top.at[z, pl.ds(1, 2)])] * 2,
+                 (top.at[zl, 1], top.at[zl, 1]),
+                 (top.at[zr, 2], top.at[zr, 2]))
     wc_z = Ring(copy, zp, zm,
                 [(wc.at[0], wc.at[3]), (wc.at[0], wc.at[1])],
                 (wc.at[3, pl.ds(0, 2)], wc.at[2, pl.ds(0, 2)]),
                 (wc.at[1, pl.ds(2, 2)], wc.at[2, pl.ds(2, 2)]))
-    wo_z = Ring(copy, zp, zm,
-                [(wo.at[x, 0], wo.at[x, 3]), (wo.at[x, 0], wo.at[x, 1])],
-                (wo.at[x, 3, pl.ds(0, 128)], wo.at[x, 2, pl.ds(0, 128)]),
-                (wo.at[x, 1, pl.ds(128, 128)], wo.at[x, 2, pl.ds(128, 128)]))
     wo_x = Ring(copy, xp, xm,
                 [(wo.at[x], wo.at[x])] * 2,
                 (wo.at[xl, pl.ds(0, 2)], wo.at[xl, pl.ds(0, 2)]),
                 (wo.at[xr, pl.ds(2, 2)], wo.at[xr, pl.ds(2, 2)]))
 
-    for one in top_go + mid_go + [wc_hop, wo_hop]:
+    for one in top_go + mid_go + wc_hop + wo_hop:
         one.start()
     for one in w_loads:
         one.start()
@@ -228,6 +219,13 @@
                 past = mid[0:2 * i]
                 parts.append((past[:, 1].reshape(i * QB, DH), with_ones(past[:, 2].reshape(i * QB, DH)), None))
             o, e = attend(now[:, 0].reshape(QB, DH), parts)
+            here = pl.ds(i * QB, QB)
+            et = extra[1, here]
+            peak = jnp.maximum(e, et)
+            fm, ft = jnp.exp2(e - peak), jnp.exp2(et - peak)
+            both = fm + ft
+            o = (o * fm + extra[0, here] * ft) / both
+            e = peak + jnp.log2(both)
             for half in range(2):
                 res_mid[2 * i + half, pl.ds(0, MID)] = o[half * MID:(half + 1) * MID].astype(BF16)
                 rest = e[half * MID:(half + 1) * MID].T[:16]
@@ -239,69 +237,53 @@
     def level2():
         row = lax.broadcasted_iota(jnp.int32, (256, 1024), 0)
         col = lax.broadcasted_iota(jnp.int32, (256, 1024), 1)
-
-        def spot(index, xx):
-            return (((index >> 6) & 3) * 8 + xx * 2 + ((index >> 5) & 1)) * TOP + (index & 31)
-
-        ok = spot(col, col >> 8) <= spot(row, x)
         key = top[:, 1].reshape(1024, DH)
         val = top[:, 2].reshape(1024, DH)
-        o, e = attend(top[x, 0].reshape(256, DH), [(key, with_ones(val), ok)])
-        for t in range(8):
-            res_top[t, 0] = o[t * TOP:(t + 1) * TOP]
-            res_top[t, 1] = e[t * TOP:(t + 1) * TOP]
+        o, e = attend(top[z, 0].reshape(256, DH), [(key, with_ones(val), col <= row + z * 256)])
+        hit = pl.ds(h, 256, stride=4)
+        extra[0, hit, :] = o
+        extra[1, hit, :] = e
 
     lax.fori_loop(0, 2, level0, 0)
     for one in top_go:
         one.wait_recv()
-    top_x.start()
-    wo_hop.wait_recv()
-    wo_z.start()
+    top_z.start()
     lax.fori_loop(2, 4, level0, 0)
+    top_z.forward()
+    for one in wc_hop:
+        one.wait_recv()
+    wc_z.start()
+    lax.fori_loop(4, 6, level0, 0)
+    top_z.finish()
+    level2()
     for one in mid_go:
         one.wait_recv()
     level1()
     for one in mid_back:
         one.start()
     ret_mid[s] = res_mid[s]
-    top_x.forward()
-    wc_hop.wait_recv()
-    wc_x.start()
-    lax.fori_loop(4, 6, level0, 0)
-    top_x.finish()
-    level2()
-    for one in top_back:
-        one.start()
-    ret_top[u] = res_top[u]
-    wc_x.forward()
-    wo_z.forward()
+    for one in wo_hop:
+        one.wait_recv()
+    wo_x.start()
     lax.fori_loop(6, 8, level0, 0)
-    wc_x.finish()
-    wc_z.start()
-
-    for one in mid_back + top_back:
-        one.wait_recv()
-    wo_z.finish()
-    wo_x.start()
+
+    for one in mid_back:
+        one.wait_recv()
 
     def late(j, carry):
-        spread[0] = jnp.zeros((MID, DH), F32)
-        spread[1] = jnp.full((MID, DH), NEG, F32)
-        hit = pl.ds(h, TOP, stride=4)
-        spread[0, hit, :] = ret_top[j, 0]
-        spread[1, hit, :] = ret_top[j, 1]
-        ea, et = aff[j, 1], spread[1]
+        ea = aff[j, 1]
         tail = [ret_mid[j, pl.ds(MID + 16 * n, 16)].astype(F32)[:1] for n in range(3)]
         em = jnp.broadcast_to(tail[0] + tail[1] + tail[2], (MID, DH)).T
-        peak = jnp.maximum(ea, jnp.maximum(em, et))
-        fa, fm, ft = jnp.exp2(ea - peak), jnp.exp2(em - peak), jnp.exp2(et - peak)
-        upper = aff[j, 0] * fa + ret_mid[j, pl.ds(0, MID)].astype(F32) * fm + spread[0] * ft
+        peak = jnp.maximum(ea, em)
+        fa, fm = jnp.exp2(ea - peak), jnp.exp2(em - peak)
+        upper = aff[j, 0] * fa + ret_mid[j, pl.ds(0, MID)].astype(F32) * fm
         attn[pl.ds(pl.multiple_of(j * MID, MID), MID), pl.ds(pl.multiple_of(j * DH, DH), DH)] = (
-            upper / (fa + fm + ft)).astype(BF16)
+            upper / (fa + fm)).astype(BF16)
         attn_send(j, j).start()
         return carry
 
     lax.fori_loop(0, HEADS_HERE, late, 0)
+    wc_z.forward()
 
     def came(n, carry):
         attn_send(lax.div(n, R_MID), lax.rem(n, R_MID)).wait_recv()
@@ -315,7 +297,6 @@
     sums = []
     for d in (0, 1, 3, 2):
         if d == 1:
-            wc_z.forward()
             wo_x.forward()
         if d == 2:
             wc_z.finish()
@@ -344,9 +325,9 @@
             stores.append(load(out.at[d], out_hbm.at[:, pl.ds(zc, 256)]))
             stores[-1].start()
 
-    for ring in (wc_x, wc_z, wo_z, wo_x, top_x):
+    for ring in (wc_z, wo_x, top_z):
         ring.drain()
-    for one in mid_go + top_go + mid_back + top_back + [wc_hop, wo_hop] + [t[2] for t in sums]:
+    for one in mid_go + top_go + mid_back + wo_hop + wc_hop + [t[2] for t in sums]:
         one.wait_send()
 
     def gone(n, carry):
@@ -375,10 +356,9 @@
             vm((4, ROWS, 256), BF16), vm((4, ROWS, 256), BF16), vm((4, ROWS, 256), BF16),
             vm((8, 3, MID, DH), BF16), vm((8, 3, TOP, DH), BF16),
             vm((8, 3, MID, DH), BF16), vm((4, 3, 8, TOP, DH), BF16),
-            vm((8, MID + 48, DH), BF16), vm((8, 2, TOP, DH), F32),
-            vm((8, MID + 48, DH), BF16), vm((8, 2, TOP, DH), F32),
+            vm((8, MID + 48, DH), BF16), vm((8, MID + 48, DH), BF16),
             vm((ROWS, DH), F32), vm((ROWS, DH), F32), vm((ROWS, DH), F32),
-            vm((8, 2, MID, DH), F32), vm((2, MID, DH), F32),
+            vm((8, 2, MID, DH), F32), vm((2, ROWS, DH), F32),
             vm((2, ROWS, DH), F32),
             pltpu.SemaphoreType.DMA((144,)), pltpu.SemaphoreType.DMA((144,)),
             pltpu.SemaphoreType.DMA((24,)),

time: 79.3 us -> 77.1 us (0.972)
  Pallas kernels: 76 us -> 73.9 us
    pallas_call x1, Pallas kernels: 76 us -> 73.9 us  [local(): pl.pallas_call(body, name='attend', out_shape=jax.ShapeDtypeStruct((ROWS,...]
where the time goes in v3:
time: 77.1 us; the launch traced here: 77 us
  Pallas kernels  73.9 us (96%)
  local copies, waits for them, and re-layouts  3.08 us (4%)
    pallas_call x1, Pallas kernels, local(): pl.pallas_call(body, name='attend', out_shape=jax.ShapeDtypeStruct((ROWS,...  73.9 us
    unnamed x1, local copies, waits for them, and re-layouts  3.08 us

profile of v3, /device:TPU:0, one launch (start us, length us, event | category | flops | bytes accessed | tf_op | source)
XLA Modules:
  0.0 77.0 jit_solution(2768640597665661901)
XLA Ops:
  0.0 73.9 %attend.1 = bf16[1024,1024]{1,0:T(8,128)(2,1)} custom-call(bf16[1024,1024]{1,0:T(8,128)(2,1)} %q_hbm.1, bf16[1024,1024]{1,0:T(8,128)(2,1)} %k_hbm.1, bf16[1024,1024]{1,0:T(8,128)(2,1)} %v_hbm.1, bf16[1024,4096]{1,0:T(8,128)(2,1)} %w_hbm.1), custom_call_target="tpu_custom_call" | custom-call | flops 15000000512 | bytes 24000000 | tf_op jit(solution)/shard_map/attend/pallas_call | solution.py:345
  73.9 3.1 %copy.6 = bf16[1024,1024]{1,0:T(8,128)(2,1)} copy(bf16[1024,1024]{1,0:T(8,128)(2,1)} %attend.1) | data formatting | bytes 4194304

commit v4 on v3

--- a/solution.py
+++ b/solution.py
@@ -157,7 +157,8 @@
                         pl.ds(pl.multiple_of(block * COLS + lax.rem(z + d, 4) * 256, 256), 256)]
 
     wc_hop = [copy(w_piece(diag, n, 0), wc.at[0, n], dp) for n in range(4)]
-    wo_hop = [copy(w_piece(pair, x, d), wo.at[x, d], dp) for d in range(4)]
+    wo_hop = [copy(w_piece(pair, x, d), wo.at[x, d], dp) for d in (0, 2)]
+    wo_z = [copy(wo.at[x, 0], wo.at[x, 3], zp), copy(wo.at[x, 0], wo.at[x, 1], zm)]
     top_z = Ring(copy, zp, zm,
                  [(top.at[z, pl.ds(1, 2)], top.at[z, pl.ds(1, 2)])] * 2,
                  (top.at[zl, 1], top.at[zl, 1]),
@@ -250,6 +251,9 @@
     top_z.start()
     lax.fori_loop(2, 4, level0, 0)
     top_z.forward()
+    wo_hop[0].wait_recv()
+    for one in wo_z:
+        one.start()
     for one in wc_hop:
         one.wait_recv()
     wc_z.start()
@@ -262,7 +266,7 @@
     for one in mid_back:
         one.start()
     ret_mid[s] = res_mid[s]
-    for one in wo_hop:
+    for one in wo_hop[1:] + wo_z:
         one.wait_recv()
     wo_x.start()
     lax.fori_loop(6, 8, level0, 0)
@@ -327,7 +331,7 @@
 
     for ring in (wc_z, wo_x, top_z):
         ring.drain()
-    for one in mid_go + top_go + mid_back + wo_hop + wc_hop + [t[2] for t in sums]:
+    for one in mid_go + top_go + mid_back + wo_hop + wo_z + wc_hop + [t[2] for t in sums]:
         one.wait_send()
 
     def gone(n, carry):

time: 77.1 us -> 74.3 us (0.964)
  Pallas kernels: 73.9 us -> 71.1 us
    pallas_call x1, Pallas kernels: 73.9 us -> 71.1 us  [local(): pl.pallas_call(body, name='attend', out_shape=jax.ShapeDtypeStruct((ROWS,...]
where the time goes in v4:
time: 74.3 us; the launch traced here: 74.2 us
  Pallas kernels  71.1 us (96%)
  local copies, waits for them, and re-layouts  3.08 us (4%)
    pallas_call x1, Pallas kernels, local(): pl.pallas_call(body, name='attend', out_shape=jax.ShapeDtypeStruct((ROWS,...  71.1 us
    unnamed x1, local copies, waits for them, and re-layouts  3.08 us

profile of v4, /device:TPU:0, one launch (start us, length us, event | category | flops | bytes accessed | tf_op | source)
XLA Modules:
  0.0 74.2 jit_solution(7274807925039116391)
XLA Ops:
  0.0 71.1 %attend.1 = bf16[1024,1024]{1,0:T(8,128)(2,1)} custom-call(bf16[1024,1024]{1,0:T(8,128)(2,1)} %q_hbm.1, bf16[1024,1024]{1,0:T(8,128)(2,1)} %k_hbm.1, bf16[1024,1024]{1,0:T(8,128)(2,1)} %v_hbm.1, bf16[1024,4096]{1,0:T(8,128)(2,1)} %w_hbm.1), custom_call_target="tpu_custom_call" | custom-call | flops 15000000512 | bytes 24000000 | tf_op jit(solution)/shard_map/attend/pallas_call | solution.py:349
  71.1 3.1 %copy.6 = bf16[1024,1024]{1,0:T(8,128)(2,1)} copy(bf16[1024,1024]{1,0:T(8,128)(2,1)} %attend.1) | data formatting | bytes 4194304
